TPU v7x, 128 devices: a whole 4x4x4 slice. The times are simulated.
128 devices in a mesh: lat: 32 (over z, x, core), lon: 4 (over y).
Axes of the slice: x: 4, y: 4, z: 4, core: 2. Of those that a mesh axis runs over, the one named last changes fastest.
Arguments:
- state: float32 [512, 1440, 256], P('lat', 'lon'), may hold values from -6 to 6
- winds: bfloat16 [512, 1440, 128], P('lat', 'lon'), may hold values from -0.44921875 to 0.44921875
- decay: float32 [4], replicated, may hold values from 0.005 to 0.5
- widths: int32 [512], replicated, may hold values from 0 to 480, as said below
Outputs:
- advected: bfloat16 [512, 1440, 256], P('lat', 'lon')
Inputs may be any that keep to these rules, and one draw needn't show every extreme that they name: widths is 0 on rows 128 to 383 and at least 1 on the other rows; the first and last rows have exactly 480.
All inputs are finite; a program needn't handle non-finite values.
Results may differ from a plain program's by a relative error of at most 0.0075.
Values may be sent and summed in bfloat16 or wider, within the bound.
A program may use at most 128 MiB of HBM per device.

v0:
```python
import functools

import jax
import jax.numpy as jnp
from jax import lax
from jax.experimental import pallas as pl
from jax.experimental.pallas import tpu as pltpu
from jax.sharding import PartitionSpec as P

STEPS = 4
HALO = 2 * STEPS
MESH = pl.DeviceIdType.MESH
F32 = jnp.float32
BF16 = jnp.bfloat16
FAR = 1.0e6


def filter_kernel(
    dims, state, winds, decay, widths, ext, wext,
    stf, low, circ, gaps, table, mat, xs, yc, ot, wide, wv, wasm, wedge, wland, easm, eedge, eland, zero,
    ld, fs, fr, rs, rr, hs, hr, wsem, els, elr, wrow_s, wrow_r, loc,
):
    bands, rows, cols, pad, levels = dims
    half = 2 * levels
    lat = lax.axis_index("lat")
    lon = lax.axis_index("lon")
    quarter = bands // 4
    polar = (lat < quarter) | (lat >= bands - quarter)
    twin = jnp.where((lat // quarter) % 2 == 0, lat + quarter, lat - quarter)
    home = jnp.where(polar, lat, twin)
    has_south = lat > 0
    has_north = lat < bands - 1

    def at(la, lo):
        return {"lat": la, "lon": lo}

    def remote(src, dst, send, recv, la, lo):
        return pltpu.make_async_remote_copy(
            src_ref=src, dst_ref=dst, send_sem=send, recv_sem=recv, device_id=at(la, lo), device_id_type=MESH
        )

    barrier = pltpu.get_barrier_semaphore()
    for k in range(4):
        pl.semaphore_signal(barrier, inc=1, device_id=at(twin, (lon + k) % 4), device_id_type=MESH)
        if k:
            pl.semaphore_signal(barrier, inc=1, device_id=at(lat, (lon + k) % 4), device_id_type=MESH)

    for side in (1, bands - 1):
        pl.semaphore_signal(barrier, inc=1, device_id=at((lat + side) % bands, lon), device_id_type=MESH)

    order = []
    for g in range(2):
        for k in (2, 1, 3, 0):
            for part in (1, 0):
                order.append((g, k, part))

    def row_of(g, k, part):
        return 8 * part + 4 * g + (lon + k) % 4

    for g, k, part in order:
        i = row_of(g, k, part)
        pltpu.make_async_copy(state.at[i], stf.at[i], ld.at[i]).start()
    pltpu.make_async_copy(winds, wv, wsem.at[0]).start()

    pl.semaphore_wait(barrier, 9)

    def forward(g, h, k, part, i):
        src = low.at[i, h]
        dst = circ.at[g, h, lon]
        return remote(src, dst, fs.at[i, h], fr.at[g, h, lon], twin if part else lat, (lon + k) % 4)

    @pl.when(polar)
    def _():
        for g in range(2):
            for h in range(2):
                for k in (2, 1, 3, 0):
                    for part in (1, 0):
                        i = row_of(g, k, part)
                        if h == 0:
                            pltpu.make_async_copy(state.at[i], stf.at[i], ld.at[i]).wait()
                            low[i, 0] = stf[i, :, :half].astype(BF16)
                            low[i, 1] = stf[i, :, half:].astype(BF16)
                        if k == 0 and part == 0:
                            pltpu.make_async_copy(low.at[i, h], circ.at[g, h, lon], fr.at[g, h, lon]).start()
                        else:
                            forward(g, h, k, part, i).start()

    pltpu.make_async_copy(winds, wv, wsem.at[0]).wait()
    wedge[0] = wv[:, 0:16, :]
    wedge[1] = wv[:, cols - 16 : cols, :]

    def wind_edge(n):
        return remote(wedge.at[n], wland.at[n], wsem.at[1 + n], wsem.at[3 + n], lat, (lon + (3 if n == 0 else 1)) % 4)

    for n in range(2):
        wind_edge(n).start()

    def state_edge(n):
        return remote(eedge.at[n], eland.at[n], els.at[n], elr.at[n], lat, (lon + (3 if n == 0 else 1)) % 4)

    @pl.when(jnp.logical_not(polar))
    def _():
        def load(i, c):
            pltpu.make_async_copy(state.at[i], stf.at[i], ld.at[i]).wait()
            for h in range(2):
                lanes = slice(h * half, (h + 1) * half)
                eedge[0, i, h] = stf[i, 0:16, lanes].astype(BF16)
                eedge[1, i, h] = stf[i, cols - 16 : cols, lanes].astype(BF16)
            return c

        lax.fori_loop(0, rows, load, 0)
        for n in range(2):
            state_edge(n).start()

    zero[...] = jnp.zeros(zero.shape, BF16)

    @pl.when(jnp.logical_not(has_south))
    def _():
        pltpu.make_async_copy(zero, ext.at[pl.ds(0, HALO)], loc.at[2]).start()
        pltpu.make_async_copy(zero.at[:, 0], wext.at[pl.ds(0, HALO)], loc.at[3]).start()

    @pl.when(jnp.logical_not(has_north))
    def _():
        pltpu.make_async_copy(zero, ext.at[pl.ds(rows + HALO, HALO)], loc.at[2]).start()
        pltpu.make_async_copy(zero.at[:, 0], wext.at[pl.ds(rows + HALO, HALO)], loc.at[3]).start()

    for n in range(2):
        wind_edge(n).wait()

    def assemble(i, c):
        wide[0, 0:8] = wland[1, i, 8:16, :].astype(F32)
        wide[0, pl.ds(8, cols)] = wv[i].astype(F32)
        wide[0, pl.ds(8 + cols, 16)] = wland[0, i].astype(F32)
        wasm[i] = wide[0].astype(BF16)
        return c

    lax.fori_loop(0, rows, assemble, 0)

    def wind_rows(n):
        if n == 0:
            return remote(wasm.at[pl.ds(0, HALO)], wext.at[pl.ds(rows + HALO, HALO)], wrow_s.at[0], wrow_r.at[1], lat - 1, lon)
        return remote(wasm.at[pl.ds(rows - HALO, HALO)], wext.at[pl.ds(0, HALO)], wrow_s.at[1], wrow_r.at[0], lat + 1, lon)

    @pl.when(has_south)
    def _():
        wind_rows(0).start()

    @pl.when(has_north)
    def _():
        wind_rows(1).start()

    wind_local = pltpu.make_async_copy(wasm, wext.at[pl.ds(HALO, rows)], loc.at[0])
    wind_local.start()

    def to_south(src, i, h):
        return remote(src, ext.at[rows + HALO + i, h], hs.at[i, h], hr.at[8 + i, h], lat - 1, lon)

    def to_north(src, i, h):
        return remote(src, ext.at[i - 8, h], hs.at[i, h], hr.at[i - 8, h], lat + 1, lon)

    state_local = pltpu.make_async_copy(easm, ext.at[pl.ds(HALO, rows)], loc.at[1])

    @pl.when(jnp.logical_not(polar))
    def _():
        for n in range(2):
            state_edge(n).wait()

        def assemble_state(i, c):
            for h in range(2):
                lanes = slice(h * half, (h + 1) * half)
                wide[h, 0:8] = eland[1, i, h, 8:16, :].astype(F32)
                wide[h, pl.ds(8, cols)] = stf[i, :, lanes]
                wide[h, pl.ds(8 + cols, 16)] = eland[0, i, h].astype(F32)
                easm[i, h] = wide[h].astype(BF16)
            return c

        lax.fori_loop(0, rows, assemble_state, 0)

        def south(i, c):
            for h in range(2):
                to_south(easm.at[i, h], i, h).start()
            return c

        def north(i, c):
            for h in range(2):
                to_north(easm.at[i, h], i, h).start()
            return c

        lax.fori_loop(0, 8, south, 0)
        lax.fori_loop(8, 16, north, 0)
        state_local.start()

    far = lax.broadcasted_iota(jnp.int32, (cols, pad), 0)
    near = lax.broadcasted_iota(jnp.int32, (cols, pad), 1)
    for d in range(4):
        apart = jnp.abs(far - near - d * cols)
        apart = jnp.minimum(apart, 4 * cols - apart).astype(F32)
        gaps[d] = jnp.where(near < cols, apart, FAR)

    def tabulate(n, c):
        f, d = n // 4, n % 4
        table[f, d] = jnp.exp(-decay[f] * gaps[d])
        return c

    lax.fori_loop(0, 16, tabulate, 0)
    for d in range(4):
        xs[d, pl.ds(pad - 32, 32)] = jnp.zeros((32, 4 * levels), BF16)

    def returned(u, k):
        g, h = u // 2, u % 2
        i = jnp.where(polar, 0, 8) + 4 * g + lon
        t = (lon + k) % 4
        return (
            remote(ot.at[u, t], ext.at[HALO + i, h], rs.at[u, k], rr.at[i, h], home, t),
            pltpu.make_async_copy(ot.at[u, t], ext.at[HALO + i, h], rr.at[i, h]),
        )

    def unit(u, c):
        g, h = u // 2, u % 2
        i = jnp.where(polar, 0, 8) + 4 * g + lon
        reach = widths[home * rows + i].astype(F32)
        for t in range(4):
            pltpu.make_async_copy(low.at[0, 0], circ.at[g, h, t], fr.at[g, h, t]).wait()
        for ff in range(2):
            f = 2 * h + ff
            total = jnp.zeros((1, 1), F32)
            for d in range(4):
                kept = jnp.where(gaps[d, 0:1] <= reach, table[f, d, 0:1], 0.0)
                total = total + jnp.sum(kept, axis=1, keepdims=True)
            scale = 1.0 / total
            for d in range(4):
                mat[d] = jnp.where(gaps[d] <= reach, table[f, d] * scale, 0.0).astype(BF16)
                xs[d, pl.ds(0, cols)] = jnp.concatenate(
                    [circ[g, h, (t + d) % 4, :, ff * levels : (ff + 1) * levels] for t in range(4)], axis=1
                )
            result = jnp.dot(mat[0], xs[0], preferred_element_type=F32)
            for d in range(1, 4):
                result = result + jnp.dot(mat[d], xs[d], preferred_element_type=F32)
            for t in range(4):
                yc[pl.ds(8 + t * cols, cols), ff * levels : (ff + 1) * levels] = result[:, t * levels : (t + 1) * levels]
        yc[0:8] = yc[pl.ds(4 * cols, 8)]
        yc[pl.ds(8 + 4 * cols, 16)] = yc[8:24]
        for t in range(4):
            ot[u, t] = yc[pl.ds(t * cols, pad)].astype(BF16)
        for k in (2, 1, 3):
            returned(u, k)[0].start()

        @pl.when(polar)
        def _():
            returned(u, 0)[1].start()

        @pl.when(jnp.logical_not(polar))
        def _():
            returned(u, 0)[0].start()

        return c

    def pass_on(u):
        g, h = u // 2, u % 2

        @pl.when(polar)
        def _():
            def south(q, c):
                i = 4 * g + q
                pltpu.make_async_copy(ot.at[0, 0], ext.at[HALO + i, h], rr.at[i, h]).wait()

                @pl.when(has_south)
                def _():
                    to_south(ext.at[HALO + i, h], i, h).start()

                return c

            def north(q, c):
                i = 8 + 4 * g + q
                pltpu.make_async_copy(ot.at[0, 0], ext.at[HALO + i, h], rr.at[i, h]).wait()

                @pl.when(has_north)
                def _():
                    to_north(ext.at[HALO + i, h], i, h).start()

                return c

            lax.fori_loop(0, 4, south, 0)
            lax.fori_loop(0, 4, north, 0)

    def stage(n, c):
        @pl.when(n < 4)
        def _():
            unit(n, 0)

        @pl.when(n >= 2)
        def _():
            pass_on(n - 2)

        return c

    lax.fori_loop(0, 6, stage, 0)

    wind_local.wait()

    @pl.when(jnp.logical_not(polar))
    def _():
        state_local.wait()

    @pl.when(polar)
    def _():
        for g in range(2):
            for h in range(2):
                for k in (2, 1, 3, 0):
                    for part in (1, 0):
                        if not (k == 0 and part == 0):
                            forward(g, h, k, part, row_of(g, k, part)).wait_send()

    def sent(u, c):
        for k in (1, 2, 3):
            returned(u, k)[0].wait_send()

        @pl.when(jnp.logical_not(polar))
        def _():
            returned(u, 0)[0].wait_send()

        return c

    lax.fori_loop(0, 4, sent, 0)

    @pl.when(has_south)
    def _():
        wind_rows(0).wait_send()
        wind_rows(1).wait_recv()

        def each(i, c):
            for h in range(2):
                to_south(ext.at[HALO + i, h], i, h).wait_send()
                to_north(ext.at[HALO + i, h], i + 8, h).wait_recv()
            return c

        lax.fori_loop(0, 8, each, 0)

    @pl.when(has_north)
    def _():
        wind_rows(1).wait_send()
        wind_rows(0).wait_recv()

        def each(i, c):
            for h in range(2):
                to_north(ext.at[HALO + i, h], i + 8, h).wait_send()
                to_south(ext.at[HALO + i, h], i, h).wait_recv()
            return c

        lax.fori_loop(0, 8, each, 0)

    @pl.when(jnp.logical_not(has_south & has_north))
    def _():
        pltpu.make_async_copy(zero, ext.at[pl.ds(0, HALO)], loc.at[2]).wait()
        pltpu.make_async_copy(zero.at[:, 0], wext.at[pl.ds(0, HALO)], loc.at[3]).wait()


def advect_kernel(dims, ext, wext, out, fields, courant, nat):
    rows, cols, seg, levels = dims
    half = 2 * levels
    r = pl.program_id(0)

    def halo_cells(level, slot, h):
        for n in range(2):
            fields[level, slot, h, n] = pltpu.roll(fields[level, slot, h, seg + n], 1, 0)
            fields[level, slot, h, seg + 2 + n] = pltpu.roll(fields[level, slot, h, 2 + n], 7, 0)

    slot = r % 8
    for h in range(2):
        nat[h] = ext[0, h].astype(F32)
        for j in range(seg):
            fields[0, slot, h, 2 + j] = nat[h, pl.ds(j, 8, stride=seg)]
        halo_cells(0, slot, h)
    nat[2] = wext[0].astype(F32)
    lane = lax.broadcasted_iota(jnp.int32, (8, half), 1)
    wslot = (r + 6) % 8
    for j in range(seg):
        both = 0.5 * nat[2, pl.ds(j, 8, stride=seg)]
        other = pltpu.roll(both, levels, 1)
        courant[wslot, 0, j] = jnp.where(lane < levels, both, other)
        courant[wslot, 1, j] = jnp.where(lane < levels, other, both)

    def part(courant_half, plus, minus, plus2, minus2, f30):
        first = (plus2 - minus2) - 8.0 * (plus - minus)
        second = 16.0 * (plus + minus) - (plus2 + minus2) - f30
        return courant_half * (first + courant_half * second)

    def step(s, c):
        i = r - 2 * s
        here = i % 8
        s2, s1, n1, n2 = ((i + 6) % 8, (i + 7) % 8, (i + 1) % 8, (i + 2) % 8)
        for j in range(seg):
            cu = courant[here, 0, j]
            cv = courant[here, 1, j]
            for h in range(2):
                f = fields[s - 1, here, h, 2 + j]
                f30 = 30.0 * f
                total = part(
                    cu, fields[s - 1, here, h, 3 + j], fields[s - 1, here, h, 1 + j],
                    fields[s - 1, here, h, 4 + j], fields[s - 1, here, h, j], f30,
                ) + part(
                    cv, fields[s - 1, n1, h, 2 + j], fields[s - 1, s1, h, 2 + j],
                    fields[s - 1, n2, h, 2 + j], fields[s - 1, s2, h, 2 + j], f30,
                )
                fields[s, here, h, 2 + j] = f + (1.0 / 6.0) * total
        for h in range(2):
            halo_cells(s, here, h)
        return c

    lax.fori_loop(1, jnp.minimum(r // 4, STEPS) + 1, step, 0)

    @pl.when(r >= 4 * STEPS)
    def _():
        done = r % 8
        for h in range(2):
            for j in range(seg):
                nat[h, pl.ds(j, 8, stride=seg)] = fields[STEPS, done, h, 2 + j]
            out[0, :, h * half : (h + 1) * half] = nat[h, pl.ds(8, cols)].astype(BF16)


def per_device(state, winds, decay, widths):
    rows, cols, chans = state.shape
    levels = winds.shape[2] // 2
    half = 2 * levels
    bands = lax.axis_size("lat")
    pad = cols + 24
    wide_rows = rows + 2 * HALO
    dma = pltpu.SemaphoreType.DMA
    hbm = pl.BlockSpec(memory_space=pl.ANY)
    smem = pl.BlockSpec(memory_space=pltpu.SMEM)
    ext, wext = pl.pallas_call(
        functools.partial(filter_kernel, (bands, rows, cols, pad, levels)),
        out_shape=(
            jax.ShapeDtypeStruct((wide_rows, 2, pad, half), BF16),
            jax.ShapeDtypeStruct((wide_rows, pad, half), BF16),
        ),
        in_specs=[hbm, hbm, smem, smem],
        out_specs=(hbm, hbm),
        scratch_shapes=[
            pltpu.VMEM((rows, cols, chans), F32),
            pltpu.VMEM((rows, 2, cols, half), BF16),
            pltpu.VMEM((2, 2, 4, cols, half), BF16),
            pltpu.VMEM((4, cols, pad), F32),
            pltpu.VMEM((4, 4, cols, pad), F32),
            pltpu.VMEM((4, cols, pad), BF16),
            pltpu.VMEM((4, pad, chans), BF16),
            pltpu.VMEM((4 * cols + 24, half), F32),
            pltpu.VMEM((4, 4, pad, half), BF16),
            pltpu.VMEM((2, pad, half), F32),
            pltpu.VMEM((rows, cols, half), BF16),
            pltpu.VMEM((rows, pad, half), BF16),
            pltpu.VMEM((2, rows, 16, half), BF16),
            pltpu.VMEM((2, rows, 16, half), BF16),
            pltpu.VMEM((rows, 2, pad, half), BF16),
            pltpu.VMEM((2, rows, 2, 16, half), BF16),
            pltpu.VMEM((2, rows, 2, 16, half), BF16),
            pltpu.VMEM((HALO, 2, pad, half), BF16),
            dma((16,)), dma((16, 2)), dma((2, 2, 4)), dma((4, 4)), dma((16, 2)), dma((16, 2)), dma((16, 2)),
            dma((5,)), dma((2,)), dma((2,)), dma((2,)), dma((2,)), dma((4,)),
        ],
        compiler_params=pltpu.CompilerParams(
            collective_id=0, has_side_effects=True, vmem_limit_bytes=56 * 2**20
        ),
        name="filter_and_halo",
    )(state, winds, decay, widths)
    seg = (cols + 2 * HALO) // 8
    return pl.pallas_call(
        functools.partial(advect_kernel, (rows, cols, seg, levels)),
        grid=(wide_rows,),
        out_shape=jax.ShapeDtypeStruct((rows, cols, chans), BF16),
        in_specs=[
            pl.BlockSpec((1, 2, pad, half), lambda r: (r, 0, 0, 0)),
            pl.BlockSpec((1, pad, half), lambda r: (jnp.maximum(r - 2, 0), 0, 0)),
        ],
        out_specs=pl.BlockSpec((1, cols, chans), lambda r: (jnp.maximum(r - 4 * STEPS, 0), 0, 0)),
        scratch_shapes=[
            pltpu.VMEM((STEPS + 1, 8, 2, seg + 4, 8, half), F32),
            pltpu.VMEM((8, 2, seg, 8, half), F32),
            pltpu.VMEM((3, pad, half), F32),
        ],
        compiler_params=pltpu.CompilerParams(vmem_limit_bytes=48 * 2**20),
        name="advect_band",
    )(ext, wext)


def solution(mesh):
    in_specs = (P("lat", "lon", None), P("lat", "lon", None), P(), P())
    out_specs = P("lat", "lon", None)
    return jax.shard_map(
        per_device, mesh=mesh, in_specs=in_specs, out_specs=out_specs, check_vma=False
    )
```

profile of v0, /device:TPU:32, one launch (start us, length us, event | category | flops | bytes accessed | tf_op | source)
XLA Modules:
  0.0 219.4 jit_solution(16416610277360034545)
XLA Ops:
  0.0 88.4 %filter_and_halo.1 = (bf16[32,2,384,128]{3,2,1,0:T(8,128)(2,1)}, bf16[32,384,128]{2,1,0:T(8,128)(2,1)}) custom-call(f32[16,360,256]{2,1,0:T(8,128)} %state.1, bf16[16,360,128]{2,1,0:T(8,128)(2,1)} %winds.1, f32[4]{0:T(128)} %decay.1, s32[512]{0:T(512)} %widths.1), custom_call_target="tpu_custom_call" | custom-call | tf_op jit(solution)/shard_map/filter_and_halo/pallas_call | solution.py:431
  88.4 0.0 copy-start
  88.4 1.9 copy-done
  90.3 129.2 %advect_band.1 = bf16[16,360,256]{2,1,0:T(8,128)(2,1)} custom-call(bf16[32,2,384,128]{3,2,1,0:T(8,128)(2,1)} %get-tuple-element.7.ext, bf16[32,384,128]{2,1,0:T(8,128)(2,1)S(1)} %copy-done), custom_call_target="tpu_custom_call" | custom-call | tf_op jit(solution)/shard_map/advect_band/pallas_call | solution.py:467
Async XLA Ops:
  88.4 1.9 copy-start
where the time goes:
time: 220 us; the launch traced here: 219 us
  Pallas kernels  218 us (99%)
    pallas_call x1, Pallas kernels, per_device(): pl.pallas_call(functools.partial(advect_kernel, (rows, cols, seg, levels)...  129 us
    pallas_call x1, Pallas kernels, per_device(): pl.pallas_call(functools.partial(filter_kernel, (bands, rows, cols, pad,...  88.4 us

commit v1 on v0

--- a/solution.py
+++ b/solution.py
@@ -355,66 +355,69 @@
         pltpu.make_async_copy(zero.at[:, 0], wext.at[pl.ds(0, HALO)], loc.at[3]).wait()
 
 
-def advect_kernel(dims, ext, wext, out, fields, courant, nat):
+def advect_kernel(dims, ext, wext, out, f0, f1, f2, f3, f4, weights, nat):
     rows, cols, seg, levels = dims
     half = 2 * levels
+    fields = (f0, f1, f2, f3, f4)
     r = pl.program_id(0)
 
-    def halo_cells(level, slot, h):
+    def halo_cells(field, slot, h):
         for n in range(2):
-            fields[level, slot, h, n] = pltpu.roll(fields[level, slot, h, seg + n], 1, 0)
-            fields[level, slot, h, seg + 2 + n] = pltpu.roll(fields[level, slot, h, 2 + n], 7, 0)
+            field[slot, h, n] = pltpu.roll(field[slot, h, seg + n], 1, 0)
+            field[slot, h, seg + 2 + n] = pltpu.roll(field[slot, h, 2 + n], 7, 0)
 
     slot = r % 8
     for h in range(2):
         nat[h] = ext[0, h].astype(F32)
         for j in range(seg):
-            fields[0, slot, h, 2 + j] = nat[h, pl.ds(j, 8, stride=seg)]
-        halo_cells(0, slot, h)
+            f0[slot, h, 2 + j] = nat[h, pl.ds(j, 8, stride=seg)]
+        halo_cells(f0, slot, h)
     nat[2] = wext[0].astype(F32)
     lane = lax.broadcasted_iota(jnp.int32, (8, half), 1)
     wslot = (r + 6) % 8
     for j in range(seg):
-        both = 0.5 * nat[2, pl.ds(j, 8, stride=seg)]
+        both = nat[2, pl.ds(j, 8, stride=seg)]
         other = pltpu.roll(both, levels, 1)
-        courant[wslot, 0, j] = jnp.where(lane < levels, both, other)
-        courant[wslot, 1, j] = jnp.where(lane < levels, other, both)
-
-    def part(courant_half, plus, minus, plus2, minus2, f30):
-        first = (plus2 - minus2) - 8.0 * (plus - minus)
-        second = 16.0 * (plus + minus) - (plus2 + minus2) - f30
-        return courant_half * (first + courant_half * second)
-
-    def step(s, c):
-        i = r - 2 * s
-        here = i % 8
-        s2, s1, n1, n2 = ((i + 6) % 8, (i + 7) % 8, (i + 1) % 8, (i + 2) % 8)
-        for j in range(seg):
-            cu = courant[here, 0, j]
-            cv = courant[here, 1, j]
-            for h in range(2):
-                f = fields[s - 1, here, h, 2 + j]
-                f30 = 30.0 * f
-                total = part(
-                    cu, fields[s - 1, here, h, 3 + j], fields[s - 1, here, h, 1 + j],
-                    fields[s - 1, here, h, 4 + j], fields[s - 1, here, h, j], f30,
-                ) + part(
-                    cv, fields[s - 1, n1, h, 2 + j], fields[s - 1, s1, h, 2 + j],
-                    fields[s - 1, n2, h, 2 + j], fields[s - 1, s2, h, 2 + j], f30,
-                )
-                fields[s, here, h, 2 + j] = f + (1.0 / 6.0) * total
-        for h in range(2):
-            halo_cells(s, here, h)
-        return c
-
-    lax.fori_loop(1, jnp.minimum(r // 4, STEPS) + 1, step, 0)
+        square = both * both
+        near = (2.0 / 3.0) * both
+        near2 = (2.0 / 3.0) * square
+        far = (1.0 / 12.0) * both
+        far2 = (1.0 / 24.0) * square
+        made = (near2 - near, far - far2, near2 + near, -far - far2)
+        for n, value in enumerate(made):
+            turned = pltpu.roll(value, levels, 1)
+            weights[wslot, j, n] = jnp.where(lane < levels, value, turned)
+            weights[wslot, j, 4 + n] = jnp.where(lane < levels, turned, value)
+        weights[wslot, j, 8] = 1.0 - 1.25 * (square + other * other)
+
+    for s in range(1, STEPS + 1):
+
+        @pl.when(r >= 4 * s)
+        def _(s=s):
+            old, new = fields[s - 1], fields[s]
+            i = r - 2 * s
+            here = i % 8
+            s2, s1, n1, n2 = ((i + 6) % 8, (i + 7) % 8, (i + 1) % 8, (i + 2) % 8)
+            for j in range(seg):
+                w = [weights[here, j, n] for n in range(9)]
+                for h in range(2):
+                    along = (w[0] * old[here, h, 3 + j] + w[1] * old[here, h, 4 + j]) + (
+                        w[2] * old[here, h, 1 + j] + w[3] * old[here, h, j]
+                    )
+                    across = (w[4] * old[n1, h, 2 + j] + w[5] * old[n2, h, 2 + j]) + (
+                        w[6] * old[s1, h, 2 + j] + w[7] * old[s2, h, 2 + j]
+                    )
+                    new[here, h, 2 + j] = w[8] * old[here, h, 2 + j] + (along + across)
+            if s < STEPS:
+                for h in range(2):
+                    halo_cells(new, here, h)
 
     @pl.when(r >= 4 * STEPS)
     def _():
         done = r % 8
         for h in range(2):
             for j in range(seg):
-                nat[h, pl.ds(j, 8, stride=seg)] = fields[STEPS, done, h, 2 + j]
+                nat[h, pl.ds(j, 8, stride=seg)] = f4[done, h, 2 + j]
             out[0, :, h * half : (h + 1) * half] = nat[h, pl.ds(8, cols)].astype(BF16)
 
 
@@ -474,8 +477,8 @@
         ],
         out_specs=pl.BlockSpec((1, cols, chans), lambda r: (jnp.maximum(r - 4 * STEPS, 0), 0, 0)),
         scratch_shapes=[
-            pltpu.VMEM((STEPS + 1, 8, 2, seg + 4, 8, half), F32),
-            pltpu.VMEM((8, 2, seg, 8, half), F32),
+            *[pltpu.VMEM((8, 2, seg + 4, 8, half), F32)] * (STEPS + 1),
+            pltpu.VMEM((8, seg, 9, 8, half), F32),
             pltpu.VMEM((3, pad, half), F32),
         ],
         compiler_params=pltpu.CompilerParams(vmem_limit_bytes=48 * 2**20),

time: 220 us -> 132 us (0.60)
  Pallas kernels: 218 us -> 130 us
    pallas_call x1, Pallas kernels: 129 us -> 41.3 us  [per_device(): pl.pallas_call(functools.partial(advect_kernel, (rows, cols, seg, levels)...]
where the time goes in v1:
time: 132 us
  Pallas kernels  130 us (98%)
  local copies, waits for them, and re-layouts  1.88 us (1%)
    pallas_call x1, Pallas kernels, per_device(): pl.pallas_call(functools.partial(filter_kernel, (bands, rows, cols, pad,...  88.4 us
    pallas_call x1, Pallas kernels, per_device(): pl.pallas_call(functools.partial(advect_kernel, (rows, cols, seg, levels)...  41.3 us

profile of v1, /device:TPU:32, one launch (start us, length us, event | category | flops | bytes accessed | tf_op | source)
XLA Modules:
  0.0 131.6 jit_solution(12989242550565074861)
XLA Ops:
  0.0 88.4 %filter_and_halo.1 = (bf16[32,2,384,128]{3,2,1,0:T(8,128)(2,1)}, bf16[32,384,128]{2,1,0:T(8,128)(2,1)}) custom-call(f32[16,360,256]{2,1,0:T(8,128)} %state.1, bf16[16,360,128]{2,1,0:T(8,128)(2,1)} %winds.1, f32[4]{0:T(128)} %decay.1, s32[512]{0:T(512)} %widths.1), custom_call_target="tpu_custom_call" | custom-call | tf_op jit(solution)/shard_map/filter_and_halo/pallas_call | solution.py:434
  88.4 0.0 copy-start
  88.4 1.9 %copy-done = bf16[32,384,128]{2,1,0:T(8,128)(2,1)S(1)} copy-done((bf16[32,384,128]{2,1,0:T(8,128)(2,1)S(1)}, bf16[32,384,128]{2,1,0:T(8,128)(2,1)}, u32[]{:S(2)}) %copy-start) | copy-done | bytes 3145752
  90.3 41.3 %advect_band.1 = bf16[16,360,256]{2,1,0:T(8,128)(2,1)} custom-call(bf16[32,2,384,128]{3,2,1,0:T(8,128)(2,1)} %get-tuple-element.7.ext, bf16[32,384,128]{2,1,0:T(8,128)(2,1)S(1)} %copy-done), custom_call_target="tpu_custom_call" | custom-call | tf_op jit(solution)/shard_map/advect_band/pallas_call | solution.py:470
Async XLA Ops:
  88.4 1.9 %copy-start = (bf16[32,384,128]{2,1,0:T(8,128)(2,1)S(1)}, bf16[32,384,128]{2,1,0:T(8,128)(2,1)}, u32[]{:S(2)}) copy-start(bf16[32,384,128]{2,1,0:T(8,128)(2,1)} %get-tuple-element.8.wext) | copy-start | bytes 9437188
